TPU v7x, 32 devices: a whole 2x2x4 slice. The times are simulated.
32 devices in a mesh: dp: 4 (over y, core), expert: 8 (over z, x).
Axes of the slice: x: 2, y: 2, z: 4, core: 2. Of those that a mesh axis runs over, the one named last changes fastest.
Arguments:
- tokens: bfloat16 [384, 7168], P('expert'), may hold values from -6 to 6
- grad_out: bfloat16 [384, 7168], P('expert'), may hold values from -6 to 6
- routes: int32 [384, 2], P('expert'), may hold values from 0 to 7, all different within a row; in each aligned block of 48 rows (0 to 47, 48 to 95, ...) at most 15 rows name the same one
- gates: bfloat16 [384, 2], P('expert'), may hold values from 0.049804688 to 0.59765625
- w_gate: bfloat16 [8, 7168, 1024], P('expert', None, 'dp'), may hold values from -0.0625 to 0.0625
- w_up: bfloat16 [8, 7168, 1024], P('expert', None, 'dp'), may hold values from -0.0625 to 0.0625
- w_down: bfloat16 [8, 1024, 7168], P('expert', 'dp'), may hold values from -0.1875 to 0.1875
Outputs:
- grad_tokens: bfloat16 [384, 7168], P('expert', 'dp')
- grad_gates: float32 [384, 2], P('expert')
- grad_w_gate: bfloat16 [8, 7168, 1024], P('expert', None, 'dp')
- grad_w_up: bfloat16 [8, 7168, 1024], P('expert', None, 'dp')
- grad_w_down: bfloat16 [8, 1024, 7168], P('expert', 'dp')
Inputs may be any that keep to these rules, and one draw needn't show every extreme that they name: `routes`: within each aligned block of 48 tokens no expert is named by more than 15 pairs, a bound that some block reaches; the 2 experts of one token differ.
All inputs are finite; a program needn't handle non-finite values.
Results may differ from a plain program's by a relative error of at most 0.02.
Values may be sent and summed in bfloat16 or wider, within the bound.
A program may use at most 128 MiB of HBM per device.

v0:
```python
import jax
import jax.numpy as jnp
from jax import lax
from jax.sharding import PartitionSpec as P


def on_device(tokens, grad_out, routes, gates, w_gate, w_up, w_down):
    experts = lax.axis_size("expert")
    groups = lax.axis_size("dp")
    tok_rows = tokens.shape[0]
    width_full = tokens.shape[1]
    top = routes.shape[1]
    cap = tok_rows * top * 5 // (experts * 4)
    slots = experts * cap
    width = width_full // groups
    flat = routes.reshape(-1)
    onehot = (flat[:, None] == jnp.arange(experts, dtype=jnp.int32)[None, :]).astype(jnp.int32)
    earlier = jnp.cumsum(onehot, axis=0) - onehot
    position = jnp.sum(earlier * onehot, axis=1)
    slot_of = (flat * cap + position).reshape(tok_rows, top)
    match = slot_of[None, :, :] == jnp.arange(slots, dtype=jnp.int32)[:, None, None]
    place = jnp.any(match, axis=2).astype(jnp.bfloat16)
    gate_slots = jnp.sum(jnp.where(match, gates.astype(jnp.float32)[None, :, :], 0.0), axis=(1, 2))
    gate_slots = gate_slots.astype(jnp.bfloat16).reshape(experts, cap)

    def fill(source):
        filled = jnp.dot(place, source, preferred_element_type=jnp.float32).astype(jnp.bfloat16)
        return filled.reshape(experts, cap, source.shape[1])

    recv_in, recv_grad, recv_gate = (
        lax.all_to_all(fill(tokens), "expert", split_axis=0, concat_axis=0, tiled=True),
        lax.all_to_all(fill(grad_out), "expert", split_axis=0, concat_axis=0, tiled=True),
        lax.all_to_all(gate_slots, "expert", split_axis=0, concat_axis=0, tiled=True),
    )
    expert_in = recv_in.reshape(slots, width_full)
    expert_grad = recv_grad.reshape(slots, width_full)
    weight_col = recv_gate.reshape(slots).astype(jnp.float32)[:, None]
    gate_mat = w_gate[0]
    up_mat = w_up[0]
    down_mat = w_down[0]
    contract_last = (((1,), (1,)), ((), ()))
    contract_first = (((0,), (0,)), ((), ()))
    pre_gate = jnp.dot(expert_in, gate_mat, preferred_element_type=jnp.float32)
    pre_up = jnp.dot(expert_in, up_mat, preferred_element_type=jnp.float32)
    sigmoid_gate = jax.nn.sigmoid(pre_gate)
    activated = pre_gate * sigmoid_gate
    hidden = activated * pre_up
    stored = hidden.astype(jnp.bfloat16)
    back = lax.dot_general(expert_grad, down_mat, contract_last, preferred_element_type=jnp.float32)
    gate_terms = jnp.sum(stored.astype(jnp.float32) * back, axis=1)
    scaled = (weight_col * hidden).astype(jnp.bfloat16)
    grad_down = lax.dot_general(
        scaled, expert_grad, contract_first, preferred_element_type=jnp.float32
    ).astype(jnp.bfloat16)
    weighted = weight_col * back
    d_up = (weighted * activated).astype(jnp.bfloat16)
    d_gate = (weighted * pre_up * sigmoid_gate * (1.0 + pre_gate * (1.0 - sigmoid_gate))).astype(
        jnp.bfloat16
    )
    grad_gate = lax.dot_general(
        expert_in, d_gate, contract_first, preferred_element_type=jnp.float32
    ).astype(jnp.bfloat16)
    grad_up = lax.dot_general(
        expert_in, d_up, contract_first, preferred_element_type=jnp.float32
    ).astype(jnp.bfloat16)
    gate_total = lax.psum(gate_terms, "dp")
    first = lax.dot_general(gate_mat, d_gate, contract_last, preferred_element_type=jnp.float32)
    summed = lax.psum_scatter(
        (
            first + lax.dot_general(up_mat, d_up, contract_last, preferred_element_type=jnp.float32)
        ).astype(jnp.bfloat16),
        "dp",
        scatter_dimension=0,
        tiled=True,
    ).astype(jnp.float32)
    rows_back, gates_back = (
        lax.all_to_all(
            summed.reshape(width, experts, cap).astype(jnp.bfloat16),
            "expert",
            split_axis=1,
            concat_axis=1,
            tiled=True,
        ).astype(jnp.float32),
        lax.all_to_all(
            gate_total.reshape(1, experts, cap).astype(jnp.bfloat16),
            "expert",
            split_axis=1,
            concat_axis=1,
            tiled=True,
        ).astype(jnp.float32),
    )
    token_grad = lax.dot_general(
        place.astype(jnp.float32),
        rows_back.reshape(width, slots),
        (((0,), (1,)), ((), ())),
        precision=lax.Precision.HIGHEST,
        preferred_element_type=jnp.float32,
    )
    gate_flat = gates_back.reshape(slots)
    grad_gates = jnp.sum(jnp.where(match, gate_flat[:, None, None], 0.0), axis=0)
    return (
        token_grad.astype(jnp.bfloat16),
        grad_gates,
        grad_gate[None],
        grad_up[None],
        grad_down[None],
    )


def solution(mesh):
    placed = (
        P("expert", None),
        P("expert", None),
        P("expert", None),
        P("expert", None),
        P("expert", None, "dp"),
        P("expert", None, "dp"),
        P("expert", "dp", None),
    )
    return jax.shard_map(
        on_device,
        mesh=mesh,
        in_specs=placed,
        out_specs=(
            P("expert", "dp"),
            P("expert", None),
            P("expert", None, "dp"),
            P("expert", None, "dp"),
            P("expert", "dp", None),
        ),
        check_vma=False,
    )
```

profile of v0, /device:TPU:0, one launch (start us, length us, event | category | flops | bytes accessed | tf_op | source)
XLA Modules:
  0.0 203.4 jit_solution(7037050256204612789)
XLA Ops:
  7.2 0.0 copy-start
  7.2 0.8 copy.32
  8.0 0.1 eq.28
  8.1 0.1 fusion.18
  8.2 0.1 reduce_window_sum.11
  8.4 0.2 select_reduce_fusion.2
  8.5 0.1 reduce_sum.39
  8.7 0.1 copy.33
  8.7 0.7 multiply_add_fusion
  9.4 0.1 fusion.17
  9.5 0.0 copy-done
  9.5 0.7 convolution_convert_fusion.3
  10.2 0.0 copy-start.3
  10.2 1.8 reshape.77
  12.1 7.3 %all-to-all-start.2 = ((bf16[8,15,7168]{2,1,0:T(8,128)(2,1)}), bf16[8,15,7168]{2,1,0:T(8,128)(2,1)}, u32[]{:S(2)}, u32[]{:S(2)}) async-start(bf16[8,15,7168]{2,1,0:T(8,128)(2,1)} %reshape.77), calls=%async_computation.2 | async-start | bytes 3670016 | tf_op jit(solution)/shard_map/all_to_all | solution.py:31
  19.3 0.0 copy-done.3
  19.3 0.7 convolution_convert_fusion.4
  20.0 1.8 reshape.75
  21.8 40.2 %all-to-all-done.2 = bf16[8,15,7168]{2,1,0:T(8,128)(2,1)} async-done(((bf16[8,15,7168]{2,1,0:T(8,128)(2,1)}), bf16[8,15,7168]{2,1,0:T(8,128)(2,1)}, u32[]{:S(2)}, u32[]{:S(2)}) %all-to-all-start.2) | async-done | bytes 1720352 | tf_op jit(solution)/shard_map/all_to_all | solution.py:31
  62.0 4.3 %all-to-all-start.1 = ((bf16[8,15,7168]{2,1,0:T(8,128)(2,1)}), bf16[8,15,7168]{2,1,0:T(8,128)(2,1)}, u32[]{:S(2)}, u32[]{:S(2)}) async-start(bf16[8,15,7168]{2,1,0:T(8,128)(2,1)} %reshape.75), calls=%async_computation.1 | async-start | bytes 3670016 | tf_op jit(solution)/shard_map/all_to_all | solution.py:32
  66.3 2.1 %reshape.78 = bf16[120,7168]{1,0:T(8,128)(2,1)S(1)} reshape(bf16[8,15,7168]{2,1,0:T(8,128)(2,1)} %all-to-all-done.2) | data formatting | bytes 3440640 | tf_op jit(solution)/shard_map/reshape | solution.py:35
  68.5 0.0 copy-start.1
  68.5 2.8 %fusion.7 = f32[120,256]{1,0:T(8,128)S(1)} fusion(bf16[120,7168]{1,0:T(8,128)(2,1)S(1)} %reshape.78, bf16[1,7168,256]{2,1,0:T(8,128)(2,1)} %param.11), kind=kOutput, calls=%fused_computation.13 | convolution fusion | flops 440401920 | bytes 5513216 | tf_op jit(solution)/shard_map/dot_general | solution.py:43
  71.3 0.3 copy-done.1
  71.6 0.7 fusion.10
  72.4 36.2 %all-to-all-done.1 = bf16[8,15,7168]{2,1,0:T(8,128)(2,1)} async-done(((bf16[8,15,7168]{2,1,0:T(8,128)(2,1)}), bf16[8,15,7168]{2,1,0:T(8,128)(2,1)}, u32[]{:S(2)}, u32[]{:S(2)}) %all-to-all-start.1) | async-done | bytes 1720352 | tf_op jit(solution)/shard_map/all_to_all | solution.py:32
  108.6 3.3 %reshape.76 = bf16[120,7168]{1,0:T(8,128)(2,1)} reshape(bf16[8,15,7168]{2,1,0:T(8,128)(2,1)} %all-to-all-done.1) | data formatting | bytes 3440640 | tf_op jit(solution)/shard_map/reshape | solution.py:36
  111.9 0.0 copy-start.4
  111.9 4.0 %multiply_reduce_fusion = (f32[120]{0:T(128)S(1)}, f32[120,256]{1,0:T(8,128)S(1)}) fusion(f32[120,256]{1,0:T(8,128)S(1)} %fusion.10, f32[120,256]{1,0:T(8,128)S(1)} %fusion.7, bf16[120,7168]{1,0:T(8,128)(2,1)} %reshape.76, bf16[1,256,7168]{2,1,0:T(8,128)(2,1)} %param.13), kind=kOutput, calls=%fused_computation.22 | convolution fusion | flops 440678272 | bytes 5759456 | tf_op jit(solution)/shard_map/dot_general | solution.py:49
  115.9 5.7 %psum.7 = bf16[120]{0:T(256)(128)(2,1)S(1)} all-reduce(f32[120]{0:T(128)S(1)} %get-tuple-element.9), channel_id=1, replica_groups=mesh['dp'=4,'expert'=8] {'dp'}, use_global_device_ids=true, to_apply=%region_6.7 | all-reduce | flops 120 | bytes 720 | tf_op jit(solution)/shard_map/psum | solution.py:66
  121.6 0.7 convert_element_type.116
  122.3 4.9 %all-to-all-start.4 = ((bf16[1,8,15]{2,0,1:T(2,128)(2,1)}), bf16[1,8,15]{2,0,1:T(2,128)(2,1)S(1)}, u32[]{:S(2)}, u32[]{:S(2)}) async-start(bf16[1,8,15]{2,0,1:T(2,128)(2,1)} %convert_element_type.116), calls=%async_computation.5 | async-start | bytes 8192 | tf_op jit(solution)/shard_map/all_to_all | solution.py:84
  127.1 0.0 reduce-scatter.2.cloned.1.call-start
  127.2 0.0 copy-done.4
  127.2 6.3 %all-to-all-done.4 = bf16[1,8,15]{2,0,1:T(2,128)(2,1)S(1)} async-done(((bf16[1,8,15]{2,0,1:T(2,128)(2,1)}), bf16[1,8,15]{2,0,1:T(2,128)(2,1)S(1)}, u32[]{:S(2)}, u32[]{:S(2)}) %all-to-all-start.4) | async-done | bytes 272 | tf_op jit(solution)/shard_map/all_to_all | solution.py:84
  133.6 0.1 reshape.81
  133.6 0.7 select_reduce_fusion
  134.4 0.1 convert_element_type.115
  134.4 8.8 %all_to_all.26 = bf16[8,1,15]{2,1,0:T(2,128)(2,1)S(1)} all-to-all(bf16[8,1,15]{2,1,0:T(2,128)(2,1)S(1)} %convert_element_type.115), channel_id=1, replica_groups=mesh['dp'=4,'expert'=8] {'expert'}, dimensions={0} | all-to-all | bytes 480 | tf_op jit(solution)/shard_map/all_to_all | solution.py:33
  143.3 0.1 reshape.80
  143.4 0.1 multiply_convert_fusion.1
  143.5 0.0 copy-start.2
  143.5 3.4 %fusion.5 = f32[120,7168]{1,0:T(8,128)S(1)} fusion(bf16[120,256]{1,0:T(8,128)(2,1)S(1)} %get-tuple-element.8, bf16[1,7168,256]{2,1,0:T(8,128)(2,1)} %param.11), kind=kOutput, calls=%fused_computation.11 | convolution fusion | flops 440401920 | bytes 7172096 | tf_op jit(solution)/shard_map/dot_general | solution.py:67
  147.0 0.0 copy-done.2
  147.0 2.5 %fusion.4 = bf16[7168,120]{0,1:T(8,128)(2,1)} fusion(f32[120,7168]{1,0:T(8,128)S(1)} %fusion.5, bf16[120,256]{1,0:T(8,128)(2,1)S(1)} %get-tuple-element.7, bf16[1,7168,256]{2,1,0:T(8,128)(2,1)S(1)} %copy-done.2), kind=kOutput, calls=%fused_computation.10 | convolution fusion | flops 442122240 | bytes 8892416 | tf_op jit(solution)/shard_map/dot_general | solution.py:70
  149.4 0.0 reduce-scatter.2.cloned.1.call-update
  149.5 25.6 %reduce-scatter.2.cloned.1.call-done = bf16[1792,120]{0,1:T(8,128)(2,1)} async-done(((bf16[7168,120]{0,1:T(8,128)(2,1)}), bf16[1792,120]{0,1:T(8,128)(2,1)}) %reduce-scatter.2.cloned.1.call-update) | async-done | bytes 430096 | tf_op jit(solution)/shard_map/reduce_scatter | solution.py:68
  175.1 1.9 convert_element_type.104
  177.0 5.5 %all-to-all-start.3 = ((bf16[1792,8,15]{0,2,1:T(8,128)(2,1)}), bf16[1792,8,15]{0,2,1:T(8,128)(2,1)S(1)}, u32[]{:S(2)}, u32[]{:S(2)}) async-start(bf16[1792,8,15]{0,2,1:T(8,128)(2,1)} %convert_element_type.104), calls=%async_computation.4 | async-start | bytes 917504 | tf_op jit(solution)/shard_map/all_to_all | solution.py:77
  182.5 4.5 %fusion.2 = bf16[1,256,7168]{2,1,0:T(8,128)(2,1)} fusion(bf16[120,7168]{1,0:T(8,128)(2,1)} %reshape.76, f32[120]{0:T(128)S(1)} %reshape.80, f32[120,256]{1,0:T(8,128)S(1)} %fusion.10, f32[120,256]{1,0:T(8,128)S(1)} %fusion.7), kind=kOutput, calls=%fused_computation.5 | convolution fusion | flops 442451968 | bytes 5636576 | tf_op jit(solution)/shard_map/dot_general | solution.py:52
  187.0 3.0 %fusion.1 = bf16[1,7168,256]{2,1,0:T(8,128)(2,1)} fusion(bf16[120,7168]{1,0:T(8,128)(2,1)S(1)} %reshape.78, bf16[120,256]{1,0:T(8,128)(2,1)S(1)} %get-tuple-element.7), kind=kOutput, calls=%fused_computation.4 | convolution fusion | flops 442236928 | bytes 5451776 | tf_op jit(solution)/shard_map/dot_general | solution.py:63
  190.0 3.0 %fusion = bf16[1,7168,256]{2,1,0:T(8,128)(2,1)} fusion(bf16[120,7168]{1,0:T(8,128)(2,1)S(1)} %reshape.78, bf16[120,256]{1,0:T(8,128)(2,1)S(1)} %get-tuple-element.8), kind=kOutput, calls=%fused_computation.3 | convolution fusion | flops 442236928 | bytes 5451776 | tf_op jit(solution)/shard_map/dot_general | solution.py:60
  193.0 2.6 %all-to-all-done.3 = bf16[1792,8,15]{0,2,1:T(8,128)(2,1)S(1)} async-done(((bf16[1792,8,15]{0,2,1:T(8,128)(2,1)}), bf16[1792,8,15]{0,2,1:T(8,128)(2,1)S(1)}, u32[]{:S(2)}, u32[]{:S(2)}) %all-to-all-start.3) | async-done | bytes 430112 | tf_op jit(solution)/shard_map/all_to_all | solution.py:77
  195.6 0.1 reshape.79
  195.7 0.9 convolution_convert_fusion.5
  (3 shorter events, 0.0 us)
Async XLA Ops:
  7.2 2.4 %copy-start = (bf16[48,7168]{1,0:T(8,128)(2,1)S(1)}, bf16[48,7168]{1,0:T(8,128)(2,1)}, u32[]{:S(2)}) copy-start(bf16[48,7168]{1,0:T(8,128)(2,1)} %param.7) | copy-start | bytes 2064388
  10.2 9.1 %copy-start.3 = (bf16[48,7168]{1,0:T(8,128)(2,1)S(1)}, bf16[48,7168]{1,0:T(8,128)(2,1)}, u32[]{:S(2)}) copy-start(bf16[48,7168]{1,0:T(8,128)(2,1)} %param.8) | copy-start | bytes 2064388
  12.1 50.0 %all-to-all-start.2 = ((bf16[8,15,7168]{2,1,0:T(8,128)(2,1)}), bf16[8,15,7168]{2,1,0:T(8,128)(2,1)}, u32[]{:S(2)}, u32[]{:S(2)}) async-start(bf16[8,15,7168]{2,1,0:T(8,128)(2,1)} %reshape.77), calls=%async_computation.2 | async-start | bytes 3670016 | tf_op jit(solution)/shard_map/all_to_all | solution.py:31
  62.0 46.6 %all-to-all-start.1 = ((bf16[8,15,7168]{2,1,0:T(8,128)(2,1)}), bf16[8,15,7168]{2,1,0:T(8,128)(2,1)}, u32[]{:S(2)}, u32[]{:S(2)}) async-start(bf16[8,15,7168]{2,1,0:T(8,128)(2,1)} %reshape.75), calls=%async_computation.1 | async-start | bytes 3670016 | tf_op jit(solution)/shard_map/all_to_all | solution.py:32
  68.5 3.1 %copy-start.1 = (bf16[1,7168,256]{2,1,0:T(8,128)(2,1)S(1)}, bf16[1,7168,256]{2,1,0:T(8,128)(2,1)}, u32[]{:S(2)}) copy-start(bf16[1,7168,256]{2,1,0:T(8,128)(2,1)} %param.12) | copy-start | bytes 11010052
  111.9 15.3 %copy-start.4 = (bf16[48,2]{0,1:T(2,128)(2,1)S(1)}, bf16[48,2]{0,1:T(2,128)(2,1)}, u32[]{:S(2)}) copy-start(bf16[48,2]{0,1:T(2,128)(2,1)} %param.10) | copy-start | bytes 580
  122.3 11.2 %all-to-all-start.4 = ((bf16[1,8,15]{2,0,1:T(2,128)(2,1)}), bf16[1,8,15]{2,0,1:T(2,128)(2,1)S(1)}, u32[]{:S(2)}, u32[]{:S(2)}) async-start(bf16[1,8,15]{2,0,1:T(2,128)(2,1)} %convert_element_type.116), calls=%async_computation.5 | async-start | bytes 8192 | tf_op jit(solution)/shard_map/all_to_all | solution.py:84
  127.1 47.9 %reduce-scatter.2.cloned.1.call-start = ((), (), s32[]{:S(2)}) async-start(), calls=%async_computation.6 | async-start | bytes 2150400 | tf_op jit(solution)/shard_map/reduce_scatter | solution.py:68
  143.5 3.5 %copy-start.2 = (bf16[1,7168,256]{2,1,0:T(8,128)(2,1)S(1)}, bf16[1,7168,256]{2,1,0:T(8,128)(2,1)}, u32[]{:S(2)}) copy-start(bf16[1,7168,256]{2,1,0:T(8,128)(2,1)} %param.12) | copy-start | bytes 11010052
  177.0 18.6 %all-to-all-start.3 = ((bf16[1792,8,15]{0,2,1:T(8,128)(2,1)}), bf16[1792,8,15]{0,2,1:T(8,128)(2,1)S(1)}, u32[]{:S(2)}, u32[]{:S(2)}) async-start(bf16[1792,8,15]{0,2,1:T(8,128)(2,1)} %convert_element_type.104), calls=%async_computation.4 | async-start | bytes 917504 | tf_op jit(solution)/shard_map/all_to_all | solution.py:77
Sparse Core Ops, SparseCore 0:
  149.6 25.4 reduce-scatter.1
where the time goes:
time: 204 us; the launch traced here: 203 us
  waiting for transfers between devices  111 us (54%)
  matrix products  26.2 us (13%)
  starting transfers between devices  22 us (11%)
  blocking collectives  14.5 us (7%)
  between operations  14.2 us (7%)
  local copies, waits for them, and re-layouts  13.6 us (7%)
  other arithmetic  2.05 us (1%)
    all_to_all x1, waiting for transfers between devices, on_device(): lax.all_to_all(fill(tokens), 'expert', split_axis=0, concat_axis=0, tiled...  40.2 us
    all_to_all x1, waiting for transfers between devices, on_device(): lax.all_to_all(fill(grad_out), 'expert', split_axis=0, concat_axis=0, til...  36.2 us
    reduce_scatter x1, waiting for transfers between devices, on_device(): lax.psum_scatter((first + lax.dot_general(up_mat, d_up, contract_last, pr...  25.6 us
    all_to_all x1, blocking collectives, on_device(): lax.all_to_all(gate_slots, 'expert', split_axis=0, concat_axis=0, tiled=T...  8.82 us
    all_to_all x1, starting transfers between devices, on_device(): lax.all_to_all(fill(tokens), 'expert', split_axis=0, concat_axis=0, tiled...  7.25 us
    all_to_all x1, waiting for transfers between devices, on_device(): lax.all_to_all(gate_total.reshape(1, experts, cap).astype(jnp.bfloat16),...  6.32 us
    psum x1, blocking collectives, on_device(): gate_total = lax.psum(gate_terms, 'dp')  5.68 us
    all_to_all x1, starting transfers between devices, on_device(): lax.all_to_all(summed.reshape(width, experts, cap).astype(jnp.bfloat16),...  5.51 us
  transfers between devices with their start and end apart: 5, of which 5 were waited for; matrix products, arithmetic and copies ran while one was open for 9% of the time, Pallas kernels for 0%

commit v1 on v0

--- a/solution.py
+++ b/solution.py
@@ -1,7 +1,29 @@
+import functools
 import jax
 import jax.numpy as jnp
 from jax import lax
 from jax.sharding import PartitionSpec as P
+
+
+def draft_sums_all(body, axis_id):
+    current_value, spare = (lax.axis_size(axis_id), lax.axis_index(axis_id))
+    n_now = body.shape[0] // current_value
+    out_arr = list(body.shape)
+    out_arr[0] = n_now
+    part_next = out_arr[0]
+    out_arr[0] = part_next * current_value
+    plain = jnp.zeros(out_arr, body.dtype)
+    for k0 in range(current_value):
+        y = lax.dynamic_slice_in_dim(body, (spare ^ k0) * n_now, n_now, axis=0)
+        if k0:
+            y = lax.ppermute(
+                y, axis_name=axis_id, perm=list(map(lambda m: (m, m ^ k0), range(current_value)))
+            )
+        plain = lax.dynamic_update_slice_in_dim(plain, y, (spare ^ k0) * part_next, axis=0)
+    return plain
+
+
+_note_terms = functools.partial(draft_sums_all, axis_id="expert")
 
 
 def on_device(tokens, grad_out, routes, gates, w_gate, w_up, w_down):
@@ -30,7 +52,7 @@
     recv_in, recv_grad, recv_gate = (
         lax.all_to_all(fill(tokens), "expert", split_axis=0, concat_axis=0, tiled=True),
         lax.all_to_all(fill(grad_out), "expert", split_axis=0, concat_axis=0, tiled=True),
-        lax.all_to_all(gate_slots, "expert", split_axis=0, concat_axis=0, tiled=True),
+        _note_terms(gate_slots),
     )
     expert_in = recv_in.reshape(slots, width_full)
     expert_grad = recv_grad.reshape(slots, width_full)

time: 204 us -> 215 us (1.054)
  waiting for transfers between devices: 111 us -> 122 us
  blocking collectives: 14.5 us -> 5.68 us
  starting transfers between devices: 22 us -> 30.2 us
    ppermute x0 -> x7, waiting for transfers between devices: none -> 10.9 us  [draft_sums_all(): lax.ppermute(y, axis_name=axis_id, perm=list(map(lambda m: (m, m ^ k0), r...]
    all_to_all x1 -> x0, blocking collectives: 8.82 us -> none  [on_device(): lax.all_to_all(gate_slots, 'expert', split_axis=0, concat_axis=0, tiled=T...]
    ppermute x0 -> x7, starting transfers between devices: none -> 8.27 us  [draft_sums_all(): lax.ppermute(y, axis_name=axis_id, perm=list(map(lambda m: (m, m ^ k0), r...]
  transfers between devices with their start and end apart: 5 -> 12, of which waited for: 5 -> 8; matrix products, arithmetic and copies ran while one was open for 9% -> 9% of each run, Pallas kernels for 0% -> 0%
where the time goes in v1:
time: 215 us; the launch traced here: 214 us
  waiting for transfers between devices  122 us (57%)
  starting transfers between devices  30.2 us (14%)
  matrix products  26.2 us (12%)
  between operations  14.3 us (7%)
  local copies, waits for them, and re-layouts  13.9 us (6%)
  blocking collectives  5.68 us (3%)
    all_to_all x1, waiting for transfers between devices, on_device(): lax.all_to_all(fill(tokens), 'expert', split_axis=0, concat_axis=0, tiled...  40.2 us
    all_to_all x1, waiting for transfers between devices, on_device(): lax.all_to_all(fill(grad_out), 'expert', split_axis=0, concat_axis=0, til...  36.2 us
    reduce_scatter x1, waiting for transfers between devices, on_device(): lax.psum_scatter((first + lax.dot_general(up_mat, d_up, contract_last, pr...  25.6 us
    ppermute x7, waiting for transfers between devices, draft_sums_all(): lax.ppermute(y, axis_name=axis_id, perm=list(map(lambda m: (m, m ^ k0), r...  10.9 us
    ppermute x7, starting transfers between devices, draft_sums_all(): lax.ppermute(y, axis_name=axis_id, perm=list(map(lambda m: (m, m ^ k0), r...  8.27 us
    all_to_all x1, starting transfers between devices, on_device(): lax.all_to_all(fill(tokens), 'expert', split_axis=0, concat_axis=0, tiled...  7.25 us
    all_to_all x1, waiting for transfers between devices, on_device(): lax.all_to_all(gate_total.reshape(1, experts, cap).astype(jnp.bfloat16),...  6.3 us
    psum x1, blocking collectives, on_device(): gate_total = lax.psum(gate_terms, 'dp')  5.68 us
  transfers between devices with their start and end apart: 12, of which 8 were waited for; matrix products, arithmetic and copies ran while one was open for 9% of the time, Pallas kernels for 0%

profile of v1, /device:TPU:0, one launch (start us, length us, event | category | flops | bytes accessed | tf_op | source)
XLA Modules:
  0.0 214.1 jit_solution(8568150451479390204)
XLA Ops:
  7.2 0.0 copy-start
  7.2 0.8 copy.30
  8.0 0.1 eq.28
  8.1 0.1 fusion.18
  8.2 0.1 reduce_window_sum.11
  8.4 0.2 select_reduce_fusion.2
  8.5 0.1 reduce_sum.39
  8.7 0.1 copy.31
  8.7 0.7 multiply_add_fusion
  9.4 0.1 fusion.17
  9.5 0.7 convolution_convert_fusion.3
  10.2 0.0 copy-start.3
  10.2 1.8 reshape.64
  12.1 7.3 %all-to-all-start.1 = ((bf16[8,15,7168]{2,1,0:T(8,128)(2,1)}), bf16[8,15,7168]{2,1,0:T(8,128)(2,1)}, u32[]{:S(2)}, u32[]{:S(2)}) async-start(bf16[8,15,7168]{2,1,0:T(8,128)(2,1)} %reshape.64), calls=%async_computation.1 | async-start | bytes 3670016 | tf_op jit(solution)/shard_map/all_to_all | solution.py:53
  19.3 0.7 convolution_convert_fusion.4
  20.0 0.0 copy-start.4
  20.0 1.8 reshape.62
  21.8 40.2 %all-to-all-done.1 = bf16[8,15,7168]{2,1,0:T(8,128)(2,1)} async-done(((bf16[8,15,7168]{2,1,0:T(8,128)(2,1)}), bf16[8,15,7168]{2,1,0:T(8,128)(2,1)}, u32[]{:S(2)}, u32[]{:S(2)}) %all-to-all-start.1) | async-done | bytes 1720352 | tf_op jit(solution)/shard_map/all_to_all | solution.py:53
  62.0 4.3 %all-to-all-start = ((bf16[8,15,7168]{2,1,0:T(8,128)(2,1)}), bf16[8,15,7168]{2,1,0:T(8,128)(2,1)}, u32[]{:S(2)}, u32[]{:S(2)}) async-start(bf16[8,15,7168]{2,1,0:T(8,128)(2,1)} %reshape.62), calls=%async_computation | async-start | bytes 3670016 | tf_op jit(solution)/shard_map/all_to_all | solution.py:54
  66.4 2.1 reshape.65
  68.5 0.0 copy-start.1
  68.5 2.9 %fusion.7 = f32[120,256]{1,0:T(8,128)S(1)} fusion(bf16[120,7168]{1,0:T(8,128)(2,1)S(1)} %reshape.65, bf16[1,7168,256]{2,1,0:T(8,128)(2,1)} %param.11), kind=kOutput, calls=%fused_computation.13 | convolution fusion | flops 440401920 | bytes 5513216 | tf_op jit(solution)/shard_map/dot_general | solution.py:65
  71.4 0.3 copy-done.1
  71.7 0.7 fusion.10
  72.4 36.2 %all-to-all-done = bf16[8,15,7168]{2,1,0:T(8,128)(2,1)} async-done(((bf16[8,15,7168]{2,1,0:T(8,128)(2,1)}), bf16[8,15,7168]{2,1,0:T(8,128)(2,1)}, u32[]{:S(2)}, u32[]{:S(2)}) %all-to-all-start) | async-done | bytes 1720352 | tf_op jit(solution)/shard_map/all_to_all | solution.py:54
  108.6 3.3 %reshape.63 = bf16[120,7168]{1,0:T(8,128)(2,1)} reshape(bf16[8,15,7168]{2,1,0:T(8,128)(2,1)} %all-to-all-done) | data formatting | bytes 3440640 | tf_op jit(solution)/shard_map/reshape | solution.py:58
  111.9 4.0 %multiply_reduce_fusion = (f32[120]{0:T(128)S(1)}, f32[120,256]{1,0:T(8,128)S(1)}) fusion(f32[120,256]{1,0:T(8,128)S(1)} %fusion.10, f32[120,256]{1,0:T(8,128)S(1)} %fusion.7, bf16[120,7168]{1,0:T(8,128)(2,1)} %reshape.63, bf16[1,256,7168]{2,1,0:T(8,128)(2,1)} %param.13), kind=kOutput, calls=%fused_computation.22 | convolution fusion | flops 440678272 | bytes 5759456 | tf_op jit(solution)/shard_map/dot_general | solution.py:71
  115.9 5.7 %psum.7 = bf16[120]{0:T(256)(128)(2,1)S(1)} all-reduce(f32[120]{0:T(128)S(1)} %get-tuple-element.17), channel_id=1, replica_groups=mesh['dp'=4,'expert'=8] {'dp'}, use_global_device_ids=true, to_apply=%region_6.7 | all-reduce | flops 120 | bytes 720 | tf_op jit(solution)/shard_map/psum | solution.py:88
  121.6 0.7 convert_element_type.108
  122.3 4.9 %all-to-all-start.3 = ((bf16[1,8,15]{2,0,1:T(2,128)(2,1)}), bf16[1,8,15]{2,0,1:T(2,128)(2,1)S(1)}, u32[]{:S(2)}, u32[]{:S(2)}) async-start(bf16[1,8,15]{2,0,1:T(2,128)(2,1)} %convert_element_type.108), calls=%async_computation.4 | async-start | bytes 8192 | tf_op jit(solution)/shard_map/all_to_all | solution.py:106
  127.1 0.0 reduce-scatter.2.cloned.1.call-start
  127.2 6.3 %all-to-all-done.3 = bf16[1,8,15]{2,0,1:T(2,128)(2,1)S(1)} async-done(((bf16[1,8,15]{2,0,1:T(2,128)(2,1)}), bf16[1,8,15]{2,0,1:T(2,128)(2,1)S(1)}, u32[]{:S(2)}, u32[]{:S(2)}) %all-to-all-start.3) | async-done | bytes 272 | tf_op jit(solution)/shard_map/all_to_all | solution.py:106
  133.5 0.1 reshape.68
  133.6 0.7 select_reduce_fusion
  134.4 0.1 convert_element_type.88
  134.5 0.6 collective-permute-start.6
  135.1 3.2 %collective-permute-start.5 = (bf16[1,15]{1,0:T(2,128)(2,1)S(1)}, bf16[1,15]{1,0:T(2,128)(2,1)S(1)}, u32[]{:S(2)}, u32[]{:S(2)}) collective-permute-start(bf16[1,15]{1,0:T(2,128)(2,1)S(1)} %get-tuple-element.10), channel_id=1, source_target_pairs={{0,6},{1,7},{2,4},{3,5},{4,2},{5,3},{6,0},{7,1},{8,14},{9,15},{10,... | collective-permute-start | bytes 98 | tf_op jit(solution)/shard_map/ppermute | solution.py:19
  138.3 0.0 collective-permute-start.4
  138.3 3.8 %collective-permute-start.3 = (bf16[1,15]{1,0:T(2,128)(2,1)S(1)}, bf16[1,15]{1,0:T(2,128)(2,1)S(1)}, u32[]{:S(2)}, u32[]{:S(2)}) collective-permute-start(bf16[1,15]{1,0:T(2,128)(2,1)S(1)} %get-tuple-element.12), channel_id=1, source_target_pairs={{0,4},{1,5},{2,6},{3,7},{4,0},{5,1},{6,2},{7,3},{8,12},{9,13},{10,... | collective-permute-start | bytes 98 | tf_op jit(solution)/shard_map/ppermute | solution.py:19
  142.2 0.6 collective-permute-start
  142.8 3.0 %collective-permute-done = bf16[1,15]{1,0:T(2,128)(2,1)S(1)} collective-permute-done((bf16[1,15]{1,0:T(2,128)(2,1)S(1)}, bf16[1,15]{1,0:T(2,128)(2,1)S(1)}, u32[]{:S(2)}, u32[]{:S(2)}) %collective-permute-start) | collective-permute-done | bytes 62 | tf_op jit(solution)/shard_map/ppermute | solution.py:19
  145.7 0.0 collective-permute-start.1
  145.8 3.5 %collective-permute-done.1 = bf16[1,15]{1,0:T(2,128)(2,1)S(1)} collective-permute-done((bf16[1,15]{1,0:T(2,128)(2,1)S(1)}, bf16[1,15]{1,0:T(2,128)(2,1)S(1)}, u32[]{:S(2)}, u32[]{:S(2)}) %collective-permute-start.1) | collective-permute-done | bytes 62 | tf_op jit(solution)/shard_map/ppermute | solution.py:19
  149.3 0.0 collective-permute-start.2
  149.3 4.4 %collective-permute-done.2 = bf16[1,15]{1,0:T(2,128)(2,1)S(1)} collective-permute-done((bf16[1,15]{1,0:T(2,128)(2,1)S(1)}, bf16[1,15]{1,0:T(2,128)(2,1)S(1)}, u32[]{:S(2)}, u32[]{:S(2)}) %collective-permute-start.2) | collective-permute-done | bytes 62 | tf_op jit(solution)/shard_map/ppermute | solution.py:19
  153.7 0.0 collective-permute-done.3
  153.8 0.0 collective-permute-done.4
  153.8 0.0 collective-permute-done.5
  153.8 0.0 collective-permute-done.6
  153.9 0.1 reshape.67
  154.0 0.1 multiply_convert_fusion.1
  154.1 0.0 copy-start.2
  154.1 3.4 %fusion.5 = f32[120,7168]{1,0:T(8,128)S(1)} fusion(bf16[120,256]{1,0:T(8,128)(2,1)S(1)} %get-tuple-element.8, bf16[1,7168,256]{2,1,0:T(8,128)(2,1)} %param.11), kind=kOutput, calls=%fused_computation.11 | convolution fusion | flops 440401920 | bytes 7172096 | tf_op jit(solution)/shard_map/dot_general | solution.py:89
  157.6 2.5 %fusion.4 = bf16[7168,120]{0,1:T(8,128)(2,1)} fusion(f32[120,7168]{1,0:T(8,128)S(1)} %fusion.5, bf16[120,256]{1,0:T(8,128)(2,1)S(1)} %get-tuple-element.7, bf16[1,7168,256]{2,1,0:T(8,128)(2,1)S(1)} %copy-done.2), kind=kOutput, calls=%fused_computation.10 | convolution fusion | flops 442122240 | bytes 8892416 | tf_op jit(solution)/shard_map/dot_general | solution.py:92
  160.0 0.0 reduce-scatter.2.cloned.1.call-update
  160.1 25.6 %reduce-scatter.2.cloned.1.call-done = bf16[1792,120]{0,1:T(8,128)(2,1)} async-done(((bf16[7168,120]{0,1:T(8,128)(2,1)}), bf16[1792,120]{0,1:T(8,128)(2,1)}) %reduce-scatter.2.cloned.1.call-update) | async-done | bytes 430096 | tf_op jit(solution)/shard_map/reduce_scatter | solution.py:90
  185.7 1.9 convert_element_type.97
  187.6 5.5 %all-to-all-start.2 = ((bf16[1792,8,15]{0,2,1:T(8,128)(2,1)}), bf16[1792,8,15]{0,2,1:T(8,128)(2,1)S(1)}, u32[]{:S(2)}, u32[]{:S(2)}) async-start(bf16[1792,8,15]{0,2,1:T(8,128)(2,1)} %convert_element_type.97), calls=%async_computation.3 | async-start | bytes 917504 | tf_op jit(solution)/shard_map/all_to_all | solution.py:99
  193.1 4.5 %fusion.2 = bf16[1,256,7168]{2,1,0:T(8,128)(2,1)} fusion(bf16[120,7168]{1,0:T(8,128)(2,1)} %reshape.63, f32[120]{0:T(128)S(1)} %reshape.67, f32[120,256]{1,0:T(8,128)S(1)} %fusion.10, f32[120,256]{1,0:T(8,128)S(1)} %fusion.7), kind=kOutput, calls=%fused_computation.5 | convolution fusion | flops 442451968 | bytes 5636576 | tf_op jit(solution)/shard_map/dot_general | solution.py:74
  197.6 3.0 %fusion.1 = bf16[1,7168,256]{2,1,0:T(8,128)(2,1)} fusion(bf16[120,7168]{1,0:T(8,128)(2,1)S(1)} %reshape.65, bf16[120,256]{1,0:T(8,128)(2,1)S(1)} %get-tuple-element.7), kind=kOutput, calls=%fused_computation.4 | convolution fusion | flops 442236928 | bytes 5451776 | tf_op jit(solution)/shard_map/dot_general | solution.py:85
  200.6 3.0 %fusion = bf16[1,7168,256]{2,1,0:T(8,128)(2,1)} fusion(bf16[120,7168]{1,0:T(8,128)(2,1)S(1)} %reshape.65, bf16[120,256]{1,0:T(8,128)(2,1)S(1)} %get-tuple-element.8), kind=kOutput, calls=%fused_computation.3 | convolution fusion | flops 442236928 | bytes 5451776 | tf_op jit(solution)/shard_map/dot_general | solution.py:82
  203.6 2.6 %all-to-all-done.2 = bf16[1792,8,15]{0,2,1:T(8,128)(2,1)S(1)} async-done(((bf16[1792,8,15]{0,2,1:T(8,128)(2,1)}), bf16[1792,8,15]{0,2,1:T(8,128)(2,1)S(1)}, u32[]{:S(2)}, u32[]{:S(2)}) %all-to-all-start.2) | async-done | bytes 430112 | tf_op jit(solution)/shard_map/all_to_all | solution.py:99
  206.2 0.1 reshape.66
  206.3 0.9 convolution_convert_fusion.5
  (16 shorter events, 0.3 us)
Async XLA Ops:
  7.2 2.4 %copy-start = (bf16[48,7168]{1,0:T(8,128)(2,1)S(1)}, bf16[48,7168]{1,0:T(8,128)(2,1)}, u32[]{:S(2)}) copy-start(bf16[48,7168]{1,0:T(8,128)(2,1)} %param.7) | copy-start | bytes 2064388
  10.2 9.1 %copy-start.3 = (bf16[48,7168]{1,0:T(8,128)(2,1)S(1)}, bf16[48,7168]{1,0:T(8,128)(2,1)}, u32[]{:S(2)}) copy-start(bf16[48,7168]{1,0:T(8,128)(2,1)} %param.8) | copy-start | bytes 2064388
  12.1 50.0 %all-to-all-start.1 = ((bf16[8,15,7168]{2,1,0:T(8,128)(2,1)}), bf16[8,15,7168]{2,1,0:T(8,128)(2,1)}, u32[]{:S(2)}, u32[]{:S(2)}) async-start(bf16[8,15,7168]{2,1,0:T(8,128)(2,1)} %reshape.64), calls=%async_computation.1 | async-start | bytes 3670016 | tf_op jit(solution)/shard_map/all_to_all | solution.py:53
  20.0 46.4 %copy-start.4 = (bf16[48,2]{0,1:T(2,128)(2,1)S(1)}, bf16[48,2]{0,1:T(2,128)(2,1)}, u32[]{:S(2)}) copy-start(bf16[48,2]{0,1:T(2,128)(2,1)} %param.10) | copy-start | bytes 580
  62.0 46.6 %all-to-all-start = ((bf16[8,15,7168]{2,1,0:T(8,128)(2,1)}), bf16[8,15,7168]{2,1,0:T(8,128)(2,1)}, u32[]{:S(2)}, u32[]{:S(2)}) async-start(bf16[8,15,7168]{2,1,0:T(8,128)(2,1)} %reshape.62), calls=%async_computation | async-start | bytes 3670016 | tf_op jit(solution)/shard_map/all_to_all | solution.py:54
  68.5 3.1 %copy-start.1 = (bf16[1,7168,256]{2,1,0:T(8,128)(2,1)S(1)}, bf16[1,7168,256]{2,1,0:T(8,128)(2,1)}, u32[]{:S(2)}) copy-start(bf16[1,7168,256]{2,1,0:T(8,128)(2,1)} %param.12) | copy-start | bytes 11010052
  122.3 11.2 %all-to-all-start.3 = ((bf16[1,8,15]{2,0,1:T(2,128)(2,1)}), bf16[1,8,15]{2,0,1:T(2,128)(2,1)S(1)}, u32[]{:S(2)}, u32[]{:S(2)}) async-start(bf16[1,8,15]{2,0,1:T(2,128)(2,1)} %convert_element_type.108), calls=%async_computation.4 | async-start | bytes 8192 | tf_op jit(solution)/shard_map/all_to_all | solution.py:106
  127.1 58.5 %reduce-scatter.2.cloned.1.call-start = ((), (), s32[]{:S(2)}) async-start(), calls=%async_computation.5 | async-start | bytes 2150400 | tf_op jit(solution)/shard_map/reduce_scatter | solution.py:90
  134.5 19.4 %collective-permute-start.6 = (bf16[1,15]{1,0:T(2,128)(2,1)S(1)}, bf16[1,15]{1,0:T(2,128)(2,1)S(1)}, u32[]{:S(2)}, u32[]{:S(2)}) collective-permute-start(bf16[1,15]{1,0:T(2,128)(2,1)S(1)} %get-tuple-element.9), channel_id=1, source_target_pairs={{0,7},{1,6},{2,5},{3,4},{4,3},{5,2},{6,1},{7,0},{8,15},{9,14},{10,... | collective-permute-start | bytes 98 | tf_op jit(solution)/shard_map/ppermute | solution.py:19
  135.1 18.7 %collective-permute-start.5 = (bf16[1,15]{1,0:T(2,128)(2,1)S(1)}, bf16[1,15]{1,0:T(2,128)(2,1)S(1)}, u32[]{:S(2)}, u32[]{:S(2)}) collective-permute-start(bf16[1,15]{1,0:T(2,128)(2,1)S(1)} %get-tuple-element.10), channel_id=1, source_target_pairs={{0,6},{1,7},{2,4},{3,5},{4,2},{5,3},{6,0},{7,1},{8,14},{9,15},{10,... | collective-permute-start | bytes 98 | tf_op jit(solution)/shard_map/ppermute | solution.py:19
  138.3 15.4 %collective-permute-start.4 = (bf16[1,15]{1,0:T(2,128)(2,1)S(1)}, bf16[1,15]{1,0:T(2,128)(2,1)S(1)}, u32[]{:S(2)}, u32[]{:S(2)}) collective-permute-start(bf16[1,15]{1,0:T(2,128)(2,1)S(1)} %get-tuple-element.11), channel_id=1, source_target_pairs={{0,5},{1,4},{2,7},{3,6},{4,1},{5,0},{6,3},{7,2},{8,13},{9,12},{10,... | collective-permute-start | bytes 98 | tf_op jit(solution)/shard_map/ppermute | solution.py:19
  138.3 15.4 %collective-permute-start.3 = (bf16[1,15]{1,0:T(2,128)(2,1)S(1)}, bf16[1,15]{1,0:T(2,128)(2,1)S(1)}, u32[]{:S(2)}, u32[]{:S(2)}) collective-permute-start(bf16[1,15]{1,0:T(2,128)(2,1)S(1)} %get-tuple-element.12), channel_id=1, source_target_pairs={{0,4},{1,5},{2,6},{3,7},{4,0},{5,1},{6,2},{7,3},{8,12},{9,13},{10,... | collective-permute-start | bytes 98 | tf_op jit(solution)/shard_map/ppermute | solution.py:19
  142.2 3.5 %collective-permute-start = (bf16[1,15]{1,0:T(2,128)(2,1)S(1)}, bf16[1,15]{1,0:T(2,128)(2,1)S(1)}, u32[]{:S(2)}, u32[]{:S(2)}) collective-permute-start(bf16[1,15]{1,0:T(2,128)(2,1)S(1)} %get-tuple-element.15), channel_id=1, source_target_pairs={{0,1},{1,0},{2,3},{3,2},{4,5},{5,4},{6,7},{7,6},{8,9},{9,8},{10,11... | collective-permute-start | bytes 98 | tf_op jit(solution)/shard_map/ppermute | solution.py:19
  145.7 3.5 %collective-permute-start.1 = (bf16[1,15]{1,0:T(2,128)(2,1)S(1)}, bf16[1,15]{1,0:T(2,128)(2,1)S(1)}, u32[]{:S(2)}, u32[]{:S(2)}) collective-permute-start(bf16[1,15]{1,0:T(2,128)(2,1)S(1)} %get-tuple-element.14), channel_id=1, source_target_pairs={{0,2},{1,3},{2,0},{3,1},{4,6},{5,7},{6,4},{7,5},{8,10},{9,11},{10,... | collective-permute-start | bytes 98 | tf_op jit(solution)/shard_map/ppermute | solution.py:19
  149.3 4.4 %collective-permute-start.2 = (bf16[1,15]{1,0:T(2,128)(2,1)S(1)}, bf16[1,15]{1,0:T(2,128)(2,1)S(1)}, u32[]{:S(2)}, u32[]{:S(2)}) collective-permute-start(bf16[1,15]{1,0:T(2,128)(2,1)S(1)} %get-tuple-element.13), channel_id=1, source_target_pairs={{0,3},{1,2},{2,1},{3,0},{4,7},{5,6},{6,5},{7,4},{8,11},{9,10},{10,... | collective-permute-start | bytes 98 | tf_op jit(solution)/shard_map/ppermute | solution.py:19
  154.1 3.5 %copy-start.2 = (bf16[1,7168,256]{2,1,0:T(8,128)(2,1)S(1)}, bf16[1,7168,256]{2,1,0:T(8,128)(2,1)}, u32[]{:S(2)}) copy-start(bf16[1,7168,256]{2,1,0:T(8,128)(2,1)} %param.12) | copy-start | bytes 11010052
  187.6 18.6 %all-to-all-start.2 = ((bf16[1792,8,15]{0,2,1:T(8,128)(2,1)}), bf16[1792,8,15]{0,2,1:T(8,128)(2,1)S(1)}, u32[]{:S(2)}, u32[]{:S(2)}) async-start(bf16[1792,8,15]{0,2,1:T(8,128)(2,1)} %convert_element_type.97), calls=%async_computation.3 | async-start | bytes 917504 | tf_op jit(solution)/shard_map/all_to_all | solution.py:99
Sparse Core Ops, SparseCore 0:
  160.2 25.4 reduce-scatter.1
